TPU v7x, 128 devices: a whole 4x4x4 slice. The times are simulated.
128 devices in a mesh: item: 16 (over z, y), code: 8 (over x, core).
Axes of the slice: x: 4, y: 4, z: 4, core: 2. Of those that a mesh axis runs over, the one named last changes fastest.
Arguments:
- residuals: float32 [256, 65536], P('code', 'item'), may hold values from -6 to 6
- codebook: float32 [256, 65536], P('item', 'code'), may hold values from -6 to 6
- item_weight: float32 [65536], P('item'), may hold values from 1 to 100
- code_capacity: float32 [65536], P('code'), may hold values from 0.25 to 4
- pairs: int32 [1024, 128], P('item', 'code'), may hold values from -1 to 127, as said below
Outputs:
- item_potential: float32 [65536], P('item')
- code_potential: float32 [65536], P('code')
Inputs may be any that keep to these rules, and one draw needn't show every extreme that they name: `pairs`: each entry is -1 (no candidate) or a code block's number within the code shard of its slot column. Within one item block and one code shard the live entries are distinct, the first slot is always live, and between 1 and 8 are live; some device holds exactly 8 live slots in every item block. Every code block is named by some item block.
All inputs are finite; a program needn't handle non-finite values.
Results may differ from a plain program's by a relative error of at most 0.0003.
Values sent between devices are 32-bit elements; how exact they have to be, the bound alone decides.
A program may use at most 128 MiB of HBM per device.

v0:
```python
import math
import jax
import jax.numpy as jnp
from jax import lax
from jax.sharding import PartitionSpec as P

BLOCK = 64
ITERS = 3
masked_score = -1e30
softness_factor = 0.1


def body(residuals, codebook, item_weight, code_capacity, pairs):
    item_columns = lax.all_gather(residuals, "code", axis=0, tiled=True)
    code_cols = lax.all_gather(codebook, "item", axis=0, tiled=True)
    embedding_width = item_columns.shape[0]
    item_count = item_columns.shape[1]
    code_count = code_cols.shape[1]
    item_blocks = item_count // BLOCK
    code_blocks = code_count // BLOCK
    logit_scale = 1.0 / (softness_factor * math.sqrt(embedding_width))
    weight_sum = lax.psum(jnp.sum(item_weight), "item")
    capacity_sum = lax.psum(jnp.sum(code_capacity), "code")
    item_logmass = jnp.log(item_weight) - jnp.log(weight_sum)
    code_logmass = jnp.log(code_capacity) - jnp.log(capacity_sum)
    is_live = pairs >= 0
    safe_ids = jnp.where(is_live, pairs, 0)
    target = jnp.where(is_live, pairs, code_blocks)
    item_split_cols = item_columns.reshape(embedding_width, item_blocks, BLOCK)
    code_column_splits = code_cols.reshape(embedding_width, code_blocks, BLOCK)
    group = math.gcd(item_blocks, 8)
    group_count = item_blocks // group

    def build_tiles(own, ids, live):
        picked = code_column_splits[:, ids, :]
        scores = (
            jnp.einsum("rbi,rbsj->bsij", own, picked, precision=lax.Precision.HIGHEST) * logit_scale
        )
        return jnp.where(live[:, :, None, None], scores, masked_score)

    reduce_fn = lambda tiles, ids, portion: tiles

    def one_group(group_index):
        start = group_index * group
        own = lax.dynamic_slice_in_dim(item_split_cols, start, group, 1)
        ids = lax.dynamic_slice_in_dim(safe_ids, start, group, 0)
        live = lax.dynamic_slice_in_dim(is_live, start, group, 0)
        portion = lax.dynamic_slice_in_dim(safe_ids, start, group, 0)
        return reduce_fn(build_tiles(own, ids, live), ids, portion)

    results = lax.map(one_group, jnp.arange(group_count, dtype=jnp.int32))
    saved_tile_blocks = results.reshape((item_blocks,) + results.shape[2:])

    def run_pass(reduce_fn, extra):
        return reduce_fn(saved_tile_blocks, safe_ids, extra)

    flat_target = target.reshape(-1)
    flat_rows = flat_target.shape[0]
    row_group = math.gcd(flat_rows, 256)
    one_hot = flat_target[:, None] == jnp.arange(code_blocks, dtype=jnp.int32)[None, :]
    one_hot_groups = one_hot.reshape(flat_rows // row_group, row_group, code_blocks)
    one_hot_float = one_hot.astype(jnp.float32)
    code_potential = jnp.zeros((code_count,), jnp.float32)
    item_potential = jnp.zeros((item_count,), jnp.float32)
    for sweep in range(ITERS):
        code_split = code_potential.reshape(code_blocks, BLOCK)

        def row_reduce(tiles, ids, portion):
            logits = tiles + code_split[ids][:, :, None, :]
            block_peak = jnp.max(logits, axis=(1, 3))
            block_total = jnp.sum(jnp.exp(logits - block_peak[:, None, :, None]), axis=(1, 3))
            return (block_peak, block_total)

        row_peak, row_total = run_pass(row_reduce, safe_ids)
        row_peak = row_peak.reshape(item_count)
        row_total = row_total.reshape(item_count)
        merged_peak = lax.pmax(row_peak, "code")
        merged_total = lax.psum(row_total * jnp.exp(row_peak - merged_peak), "code")
        item_potential = item_logmass - (merged_peak + jnp.log(merged_total))
        item_split = item_potential.reshape(item_blocks, BLOCK)

        def col_reduce(tiles, ids, portion):
            logits = tiles + portion[:, None, :, None]
            block_peak = jnp.max(logits, axis=2)
            block_total = jnp.sum(jnp.exp(logits - block_peak[:, :, None, :]), axis=2)
            return (block_peak, block_total)

        tile_peak, tile_total = run_pass(col_reduce, item_split)
        peak_flat = tile_peak.reshape(flat_rows, BLOCK)
        total_flat = tile_total.reshape(flat_rows, BLOCK)
        peak_groups = peak_flat.reshape(flat_rows // row_group, row_group, BLOCK)

        def peak_step(carry, pieces):
            hot, peaks = pieces
            candidate = jnp.max(jnp.where(hot[:, :, None], peaks[:, None, :], masked_score), axis=0)
            return (jnp.maximum(carry, candidate), None)

        col_peak, unused = lax.scan(
            peak_step,
            jnp.full((code_blocks, BLOCK), masked_score, jnp.float32),
            (one_hot_groups, peak_groups),
        )
        padded_peak = jnp.concatenate(
            [col_peak, jnp.full((1, BLOCK), masked_score, jnp.float32)], axis=0
        )
        spread = total_flat * jnp.exp(peak_flat - padded_peak[flat_target])
        col_total = jnp.dot(
            one_hot_float.T,
            spread,
            precision=lax.Precision.HIGHEST,
            preferred_element_type=jnp.float32,
        )
        col_peak = col_peak.reshape(code_count)
        col_total = col_total.reshape(code_count)
        joined_peak = lax.pmax(col_peak, "item")
        joined_total = lax.psum(col_total * jnp.exp(col_peak - joined_peak), "item")
        code_potential = code_logmass - (joined_peak + jnp.log(joined_total))
    return (item_potential, code_potential)


def solution(mesh):
    placed = (P("code", "item"), P("item", "code"), P("item"), P("code"), P("item", "code"))
    return jax.shard_map(
        body, mesh=mesh, in_specs=placed, out_specs=(P("item"), P("code")), check_vma=False
    )
```

profile of v0, /device:TPU:0, one launch (start us, length us, event | category | flops | bytes accessed | tf_op | source)
XLA Modules:
  0.0 1095.6 jit_solution(9727637983515556993)
XLA Ops:
  10.0 42.6 %psum.56 = f32[]{:T(128)} all-reduce(f32[]{:T(128)} %reduce_sum.72), channel_id=1, replica_groups=mesh['item'=16,'code'=8] {'item'}, use_global_device_ids=true, to_apply=%region_1.0 | all-reduce | flops 1 | bytes 8 | tf_op jit(solution)/shard_map/psum | solution.py:22
  58.9 5.6 copy.31
  64.6 52.7 %all-gather.3.cloned.1.call-done = f32[256,8192]{1,0:T(8,128)} async-done(((f32[16,8192]{1,0:T(8,128)}), f32[256,8192]{1,0:T(8,128)}) %all-gather.3.cloned.1.call-update) | async-done | bytes 8388624 | tf_op jit(solution)/shard_map/all_gather | solution.py:15
  117.3 9.0 copy.30
  126.3 158.7 %while.43 = (s32[]{:T(128)}, f32[8,8,16,64,64]{3,4,2,1,0:T(8,128)}, s32[8]{0:T(128)S(1)}, pred[64,16]{1,0:T(8,128)(4,1)S(1)}, s32[64,16]{1,0:T(8,128)S(1)}, /*in...) while((s32[]{:T(128)}, f32[8,8,16,64,64]{3,4,2,1,0:T(8,128)}, ...), condition=%wide.region_3.0_spmd, body=%wide.region_2.0_spmd.sunk | while | flops 1611662720 | bytes 29892660 | solution.py:51
  127.5 7.7 gather_fusion
  135.2 11.0 bitcast_dynamic-update-slice_fusion.2
  147.3 7.7 gather_fusion
  155.0 11.0 %bitcast_dynamic-update-slice_fusion.2 = f32[8,8,16,64,64]{3,4,2,1,0:T(8,128)} fusion(f32[8,8,16,64,64]{3,4,2,1,0:T(8,128)} %get-tuple-element.327, s32[]{:T(128)} %get-tuple-element.326, f32[256,8,16,64]{0,3,2,1:T(8,128)} %bitcast.84, pred[8,16]{1,0:T(8,128)(4,1)S(1)} %constant_dynamic-slice_fusion.2, f32[256,64,64]{0,2,1:T(8,128)} %get-tuple-element.343, ...), kind=kOutput, calls=%fused_computation.7.clone.1 | convolution fusion | flops 1611661312 | bytes 13107844 | tf_op jit(solution)/shard_map/while/body/eval_jaxpr/rbi,rbsj->bsij/dot_general | solution.py:37
  167.2 7.7 gather_fusion
  174.8 10.9 bitcast_dynamic-update-slice_fusion.2
  187.0 7.7 gather_fusion
  194.7 10.9 bitcast_dynamic-update-slice_fusion.2
  206.8 7.7 gather_fusion
  214.5 11.0 bitcast_dynamic-update-slice_fusion.2
  226.7 7.7 gather_fusion
  234.3 11.0 %bitcast_dynamic-update-slice_fusion.2 = f32[8,8,16,64,64]{3,4,2,1,0:T(8,128)} fusion(f32[8,8,16,64,64]{3,4,2,1,0:T(8,128)} %get-tuple-element.327, s32[]{:T(128)} %get-tuple-element.326, f32[256,8,16,64]{0,3,2,1:T(8,128)} %bitcast.84, pred[8,16]{1,0:T(8,128)(4,1)S(1)} %constant_dynamic-slice_fusion.2, f32[256,64,64]{0,2,1:T(8,128)} %get-tuple-element.343, ...), kind=kOutput, calls=%fused_computation.7.clone.1 | convolution fusion | flops 1611661312 | bytes 13107844 | tf_op jit(solution)/shard_map/while/body/eval_jaxpr/rbi,rbsj->bsij/dot_general | solution.py:37
  246.5 7.7 gather_fusion
  254.2 10.9 bitcast_dynamic-update-slice_fusion.2
  266.3 7.7 gather_fusion
  274.0 11.0 %bitcast_dynamic-update-slice_fusion.2 = f32[8,8,16,64,64]{3,4,2,1,0:T(8,128)} fusion(f32[8,8,16,64,64]{3,4,2,1,0:T(8,128)} %get-tuple-element.327, s32[]{:T(128)} %get-tuple-element.326, f32[256,8,16,64]{0,3,2,1:T(8,128)} %bitcast.84, pred[8,16]{1,0:T(8,128)(4,1)S(1)} %constant_dynamic-slice_fusion.2, f32[256,64,64]{0,2,1:T(8,128)} %get-tuple-element.343, ...), kind=kOutput, calls=%fused_computation.7.clone.1 | convolution fusion | flops 1611661312 | bytes 13107844 | tf_op jit(solution)/shard_map/while/body/eval_jaxpr/rbi,rbsj->bsij/dot_general | solution.py:37
  285.0 11.8 %add_reduce_fusion.5 = f32[8,8,64]{2,1,0:T(8,128)S(1)} fusion(f32[8,8,16,64,64]{3,4,2,1,0:T(8,128)} %get-tuple-element.105, f32[8,8,16,64]{3,2,1,0:T(8,128)S(1)} %bitcast.93), kind=kLoop, calls=%fused_computation.37 | loop fusion | flops 8384512 | bytes 17055744 | tf_op jit(solution)/shard_map/reduce_max | solution.py:70
  296.8 11.9 %exponential_reduce_fusion.5 = f32[8,8,64]{2,1,0:T(8,128)S(1)} fusion(f32[8,8,16,64,64]{3,4,2,1,0:T(8,128)} %get-tuple-element.105, f32[8,8,64]{2,1,0:T(8,128)S(1)} %add_reduce_fusion.5, f32[8,8,16,64]{3,2,1,0:T(8,128)S(1)} %bitcast.94), kind=kLoop, calls=%fused_computation.31 | loop fusion | flops 12578816 | bytes 17072128 | tf_op jit(solution)/shard_map/reduce_sum | solution.py:71
  308.9 25.5 %pmax.42 = f32[4096]{0:T(1024)S(1)} all-reduce(f32[4096]{0:T(1024)S(1)} %reshape.211), channel_id=1, replica_groups=mesh['item'=16,'code'=8] {'code'}, use_global_device_ids=true, to_apply=%region_7.8 | all-reduce | flops 4096 | bytes 32768 | tf_op jit(solution)/shard_map/pmax | solution.py:77
  334.4 24.6 %all-reduce.3 = (f32[4096]{0:T(1024)S(1)}, f32[]{:T(128)}) all-reduce(f32[4096]{0:T(1024)S(1)} %exponential_multiply_fusion.5, f32[]{:T(128)} %reduce_sum.73), channel_id=1, replica_groups=mesh['item'=16,'code'=8] {'code'}, use_global_device_ids=true, to_apply=%region_9.10 | all-reduce | flops 4097 | bytes 32776 | tf_op jit(solution)/shard_map/psum | solution.py:78
  359.1 15.3 %add_reduce_fusion.4 = f32[8,8,16,64]{3,2,1,0:T(8,128)S(1)} fusion(f32[8,8,16,64,64]{3,4,2,1,0:T(8,128)} %get-tuple-element.105, f32[8,8,64]{2,1,0:T(8,128)S(1)} %add.154), kind=kLoop, calls=%fused_computation.36 | loop fusion | flops 8323072 | bytes 17055744 | tf_op jit(solution)/shard_map/reduce_max | solution.py:84
  374.4 20.7 %exponential_reduce_fusion.4 = f32[8,8,16,64]{3,2,1,0:T(8,128)S(1)} fusion(f32[8,8,16,64,64]{3,4,2,1,0:T(8,128)} %get-tuple-element.105, f32[8,8,16,64]{3,2,1,0:T(8,128)S(1)} %add_reduce_fusion.4, f32[8,8,64]{2,1,0:T(8,128)S(1)} %add.154), kind=kLoop, calls=%fused_computation.30 | loop fusion | flops 12517376 | bytes 17317888 | tf_op jit(solution)/shard_map/reduce_sum | solution.py:85
  395.1 13.3 %while.44 = (s32[]{:T(128)}, f32[128,64]{0,1:T(8,128)S(1)}, pred[4,256,128]{2,1,0:T(8,128)(4,1)S(1)}, f32[4,256,64]{2,1,0:T(8,128)S(1)}, s32[]{:T(128)}, /*index=5*/s32[]{:T(128)}) while((s32[]{:T(128)}, f32[128,64]{0,1:T(8,128)S(1)}, pred[4,256,128]{2,1,0:T(8,128)(4,1)S(1)}, f32[4,256,64]{2,1,0:T(8,128)S(1)}, s32[]{:T(128)}, ...), condition=%wide.region_13.14_spmd.clone, body=%wide.region_11.13_spmd.clone.sunk | while | flops 4202499 | bytes 426071 | solution.py:98
  412.4 72.4 %pmax.43 = f32[8192]{0:T(1024)S(1)} all-reduce(f32[8192]{0:T(1024)S(1)} %reshape.213), channel_id=1, replica_groups=mesh['item'=16,'code'=8] {'item'}, use_global_device_ids=true, to_apply=%region_14.15 | all-reduce | flops 8192 | bytes 65536 | tf_op jit(solution)/shard_map/pmax | solution.py:115
  484.8 69.5 %psum.59 = f32[8192]{0:T(1024)S(1)} all-reduce(f32[8192]{0:T(1024)S(1)} %exponential_multiply_fusion.2), channel_id=1, replica_groups=mesh['item'=16,'code'=8] {'item'}, use_global_device_ids=true, to_apply=%region_16.17 | all-reduce | flops 8192 | bytes 65536 | tf_op jit(solution)/shard_map/psum | solution.py:116
  558.0 11.8 %add_reduce_fusion.3 = f32[8,8,64]{2,1,0:T(8,128)S(1)} fusion(f32[8,8,16,64,64]{3,4,2,1,0:T(8,128)} %get-tuple-element.105, f32[8,8,16,64]{3,2,1,0:T(8,128)S(1)} %bitcast.97), kind=kLoop, calls=%fused_computation.35 | loop fusion | flops 8384512 | bytes 17055744 | tf_op jit(solution)/shard_map/reduce_max | solution.py:70
  569.8 11.9 %exponential_reduce_fusion.3 = f32[8,8,64]{2,1,0:T(8,128)S(1)} fusion(f32[8,8,16,64,64]{3,4,2,1,0:T(8,128)} %get-tuple-element.105, f32[8,8,64]{2,1,0:T(8,128)S(1)} %add_reduce_fusion.3, f32[8,8,16,64]{3,2,1,0:T(8,128)S(1)} %bitcast.98), kind=kLoop, calls=%fused_computation.29 | loop fusion | flops 12578816 | bytes 17072128 | tf_op jit(solution)/shard_map/reduce_sum | solution.py:71
  581.9 23.5 %pmax.44 = f32[4096]{0:T(1024)S(1)} all-reduce(f32[4096]{0:T(1024)S(1)} %reshape.219), channel_id=1, replica_groups=mesh['item'=16,'code'=8] {'code'}, use_global_device_ids=true, to_apply=%region_18.19 | all-reduce | flops 4096 | bytes 32768 | tf_op jit(solution)/shard_map/pmax | solution.py:77
  605.4 23.6 %psum.60 = f32[4096]{0:T(1024)S(1)} all-reduce(f32[4096]{0:T(1024)S(1)} %exponential_multiply_fusion.4), channel_id=1, replica_groups=mesh['item'=16,'code'=8] {'code'}, use_global_device_ids=true, to_apply=%region_20.21 | all-reduce | flops 4096 | bytes 32768 | tf_op jit(solution)/shard_map/psum | solution.py:78
  629.1 15.3 %add_reduce_fusion.2 = f32[8,8,16,64]{3,2,1,0:T(8,128)S(1)} fusion(f32[8,8,16,64,64]{3,4,2,1,0:T(8,128)} %get-tuple-element.105, f32[8,8,64]{2,1,0:T(8,128)S(1)} %add.163), kind=kLoop, calls=%fused_computation.34 | loop fusion | flops 8323072 | bytes 17055744 | tf_op jit(solution)/shard_map/reduce_max | solution.py:84
  644.4 20.7 %exponential_reduce_fusion.2 = f32[8,8,16,64]{3,2,1,0:T(8,128)S(1)} fusion(f32[8,8,16,64,64]{3,4,2,1,0:T(8,128)} %get-tuple-element.105, f32[8,8,16,64]{3,2,1,0:T(8,128)S(1)} %add_reduce_fusion.2, f32[8,8,64]{2,1,0:T(8,128)S(1)} %add.163), kind=kLoop, calls=%fused_computation.28 | loop fusion | flops 12517376 | bytes 17317888 | tf_op jit(solution)/shard_map/reduce_sum | solution.py:85
  665.0 13.3 %while.45 = (s32[]{:T(128)}, f32[128,64]{0,1:T(8,128)S(1)}, pred[4,256,128]{2,1,0:T(8,128)(4,1)S(1)}, f32[4,256,64]{2,1,0:T(8,128)S(1)}, s32[]{:T(128)}, /*index=5*/s32[]{:T(128)}) while((s32[]{:T(128)}, f32[128,64]{0,1:T(8,128)S(1)}, pred[4,256,128]{2,1,0:T(8,128)(4,1)S(1)}, f32[4,256,64]{2,1,0:T(8,128)S(1)}, s32[]{:T(128)}, ...), condition=%wide.region_24.25_spmd.clone, body=%wide.region_22.24_spmd.clone.sunk | while | flops 4202499 | bytes 426071 | solution.py:98
  682.3 69.6 %pmax.45 = f32[8192]{0:T(1024)S(1)} all-reduce(f32[8192]{0:T(1024)S(1)} %reshape.221), channel_id=1, replica_groups=mesh['item'=16,'code'=8] {'item'}, use_global_device_ids=true, to_apply=%region_25.26 | all-reduce | flops 8192 | bytes 65536 | tf_op jit(solution)/shard_map/pmax | solution.py:115
  751.9 69.5 %psum.61 = f32[8192]{0:T(1024)S(1)} all-reduce(f32[8192]{0:T(1024)S(1)} %exponential_multiply_fusion.1), channel_id=1, replica_groups=mesh['item'=16,'code'=8] {'item'}, use_global_device_ids=true, to_apply=%region_27.28 | all-reduce | flops 8192 | bytes 65536 | tf_op jit(solution)/shard_map/psum | solution.py:116
  824.4 11.8 %add_reduce_fusion.1 = f32[8,8,64]{2,1,0:T(8,128)S(1)} fusion(f32[8,8,16,64,64]{3,4,2,1,0:T(8,128)} %get-tuple-element.105, f32[8,8,16,64]{3,2,1,0:T(8,128)S(1)} %bitcast.95), kind=kLoop, calls=%fused_computation.33 | loop fusion | flops 8384512 | bytes 17055744 | tf_op jit(solution)/shard_map/reduce_max | solution.py:70
  836.2 11.9 %exponential_reduce_fusion.1 = f32[8,8,64]{2,1,0:T(8,128)S(1)} fusion(f32[8,8,16,64,64]{3,4,2,1,0:T(8,128)} %get-tuple-element.105, f32[8,8,64]{2,1,0:T(8,128)S(1)} %add_reduce_fusion.1, f32[8,8,16,64]{3,2,1,0:T(8,128)S(1)} %bitcast.96), kind=kLoop, calls=%fused_computation.27 | loop fusion | flops 12578816 | bytes 17072128 | tf_op jit(solution)/shard_map/reduce_sum | solution.py:71
  848.3 23.5 %pmax.46 = f32[4096]{0:T(1024)S(1)} all-reduce(f32[4096]{0:T(1024)S(1)} %reshape.226), channel_id=1, replica_groups=mesh['item'=16,'code'=8] {'code'}, use_global_device_ids=true, to_apply=%region_29.30 | all-reduce | flops 4096 | bytes 32768 | tf_op jit(solution)/shard_map/pmax | solution.py:77
  871.8 23.8 %psum.62 = f32[4096]{0:T(1024)S(1)} all-reduce(f32[4096]{0:T(1024)S(1)} %exponential_multiply_fusion.3), channel_id=1, replica_groups=mesh['item'=16,'code'=8] {'code'}, use_global_device_ids=true, to_apply=%region_31.32 | all-reduce | flops 4096 | bytes 32768 | tf_op jit(solution)/shard_map/psum | solution.py:78
  895.7 15.3 %add_reduce_fusion = f32[8,8,16,64]{3,2,1,0:T(8,128)S(1)} fusion(f32[8,8,16,64,64]{3,4,2,1,0:T(8,128)} %get-tuple-element.105, f32[8,8,64]{2,1,0:T(8,128)S(1)} %add.171), kind=kLoop, calls=%fused_computation.32 | loop fusion | flops 8323072 | bytes 17055744 | tf_op jit(solution)/shard_map/reduce_max | solution.py:84
  911.0 20.7 %exponential_reduce_fusion = f32[8,8,16,64]{3,2,1,0:T(8,128)S(1)} fusion(f32[8,8,16,64,64]{3,4,2,1,0:T(8,128)} %get-tuple-element.105, f32[8,8,16,64]{3,2,1,0:T(8,128)S(1)} %add_reduce_fusion, f32[8,8,64]{2,1,0:T(8,128)S(1)} %add.171), kind=kLoop, calls=%fused_computation.26 | loop fusion | flops 12517376 | bytes 17317888 | tf_op jit(solution)/shard_map/reduce_sum | solution.py:85
  931.7 13.3 %while.46 = (s32[]{:T(128)}, f32[128,64]{0,1:T(8,128)S(1)}, pred[4,256,128]{2,1,0:T(8,128)(4,1)S(1)}, f32[4,256,64]{2,1,0:T(8,128)S(1)}, s32[]{:T(128)}, /*index=5*/s32[]{:T(128)}) while((s32[]{:T(128)}, f32[128,64]{0,1:T(8,128)S(1)}, pred[4,256,128]{2,1,0:T(8,128)(4,1)S(1)}, f32[4,256,64]{2,1,0:T(8,128)S(1)}, s32[]{:T(128)}, ...), condition=%wide.region_35.36_spmd.clone, body=%wide.region_33.35_spmd.clone.sunk | while | flops 4202499 | bytes 426071 | solution.py:98
  948.9 69.6 %pmax.47 = f32[8192]{0:T(1024)S(1)} all-reduce(f32[8192]{0:T(1024)S(1)} %reshape.228), channel_id=1, replica_groups=mesh['item'=16,'code'=8] {'item'}, use_global_device_ids=true, to_apply=%region_36.37 | all-reduce | flops 8192 | bytes 65536 | tf_op jit(solution)/shard_map/pmax | solution.py:115
  1018.5 69.5 %psum.63 = f32[8192]{0:T(1024)S(1)} all-reduce(f32[8192]{0:T(1024)S(1)} %exponential_multiply_fusion), channel_id=1, replica_groups=mesh['item'=16,'code'=8] {'item'}, use_global_device_ids=true, to_apply=%region_38.39 | all-reduce | flops 8192 | bytes 65536 | tf_op jit(solution)/shard_map/psum | solution.py:116
  (169 shorter events, 71.9 us)
Async XLA Ops:
  7.2 51.8 %all-gather.5.cloned.1.call-start = ((), (), s32[]{:S(2)}) async-start(), calls=%async_computation.1 | async-start | bytes 4718592 | tf_op jit(solution)/shard_map/all_gather | solution.py:14
  7.9 109.4 %all-gather.3.cloned.1.call-start = ((), (), s32[]{:S(2)}) async-start(), calls=%async_computation | async-start | bytes 8912896 | tf_op jit(solution)/shard_map/all_gather | solution.py:15
  285.0 74.0 %copy-start.3 = (f32[4096]{0:T(1024)S(1)}, f32[4096]{0:T(1024)}, u32[]{:S(2)}) copy-start(f32[4096]{0:T(1024)} %param.15) | copy-start | bytes 49156
  359.1 195.9 %copy-start.2 = (f32[8192]{0:T(1024)S(1)}, f32[8192]{0:T(1024)}, u32[]{:S(2)}) copy-start(f32[8192]{0:T(1024)} %param.16) | copy-start | bytes 98308
  629.1 36.0 %copy-start.1 = (f32[128,64]{0,1:T(8,128)S(1)}, f32[128,64]{0,1:T(8,128)}, u32[]{:S(2)}) copy-start(f32[128,64]{0,1:T(8,128)} %custom-call.1) | copy-start | bytes 98308
  895.6 36.1 %copy-start.4 = (f32[4096]{0:T(1024)}, f32[4096]{0:T(1024)S(1)}, u32[]{:S(2)}) copy-start(f32[4096]{0:T(1024)S(1)} %add_subtract_fusion.3) | copy-start | bytes 49156
  895.7 36.0 %copy-start = (f32[128,64]{0,1:T(8,128)S(1)}, f32[128,64]{0,1:T(8,128)}, u32[]{:S(2)}) copy-start(f32[128,64]{0,1:T(8,128)} %custom-call.2) | copy-start | bytes 98308
Sparse Core Ops, SparseCore 0:
  9.7 34.5 all-gather.4
  46.4 70.8 all-gather.2
where the time goes:
time: 1100 us
  blocking collectives  607 us (55%)
  other arithmetic  222 us (20%)
  local copies, waits for them, and re-layouts  101 us (9%)
  matrix products  89.9 us (8%)
  waiting for transfers between devices  54.1 us (5%)
  between operations  15.8 us (1%)
    pmax x3, blocking collectives, body(): joined_peak = lax.pmax(col_peak, 'item')  212 us
    psum x3, blocking collectives, body(): joined_total = lax.psum(col_total * jnp.exp(col_peak - joined_peak), 'item')  209 us
    dot_general x8, matrix products, build_tiles(): jnp.einsum('rbi,rbsj->bsij', own, picked, precision=lax.Precision.HIGHEST)  87.6 us
    pmax x3, blocking collectives, body(): merged_peak = lax.pmax(row_peak, 'code')  72.6 us
    psum x3, blocking collectives, body(): merged_total = lax.psum(row_total * jnp.exp(row_peak - merged_peak), 'code')  71.9 us
    reduce_sum x3, other arithmetic, col_reduce(): block_total = jnp.sum(jnp.exp(logits - block_peak[:, :, None, :]), axis=2)  62 us
    gather x8, local copies, waits for them, and re-layouts, build_tiles(): picked = code_column_splits[:, ids, :]  61.3 us
    all_gather x1, waiting for transfers between devices, body(): code_cols = lax.all_gather(codebook, 'item', axis=0, tiled=True)  52.7 us
  transfers between devices with their start and end apart: 2, of which 1 were waited for; matrix products, arithmetic and copies ran while one was open for 1% of the time, Pallas kernels for 0%

commit v1 on v0

--- a/solution.py
+++ b/solution.py
@@ -113,7 +113,8 @@
         col_peak = col_peak.reshape(code_count)
         col_total = col_total.reshape(code_count)
         joined_peak = lax.pmax(col_peak, "item")
-        joined_total = lax.psum(col_total * jnp.exp(col_peak - joined_peak), "item")
+        block_in = col_total * jnp.exp(col_peak - joined_peak)
+        joined_total = lax.all_gather(block_in, "item").sum(axis=0)
         code_potential = code_logmass - (joined_peak + jnp.log(joined_total))
     return (item_potential, code_potential)
 

time: 1100 us -> 957 us (0.87)
  blocking collectives: 607 us -> 466 us
    psum x3 -> x0, blocking collectives: 209 us -> none  [body(): joined_total = lax.psum(col_total * jnp.exp(col_peak - joined_peak), 'item')]
    all_gather x0 -> x3, blocking collectives: none -> 62.8 us  [body(): joined_total = lax.all_gather(block_in, 'item').sum(axis=0)]
where the time goes in v1:
time: 957 us; the launch traced here: 955 us
  blocking collectives  466 us (49%)
  other arithmetic  223 us (23%)
  local copies, waits for them, and re-layouts  101 us (11%)
  matrix products  89.9 us (9%)
  waiting for transfers between devices  54.1 us (6%)
  between operations  15.8 us (2%)
    pmax x3, blocking collectives, body(): joined_peak = lax.pmax(col_peak, 'item')  217 us
    dot_general x8, matrix products, build_tiles(): jnp.einsum('rbi,rbsj->bsij', own, picked, precision=lax.Precision.HIGHEST)  87.6 us
    pmax x3, blocking collectives, body(): merged_peak = lax.pmax(row_peak, 'code')  72.6 us
    psum x3, blocking collectives, body(): merged_total = lax.psum(row_total * jnp.exp(row_peak - merged_peak), 'code')  71.9 us
    all_gather x3, blocking collectives, body(): joined_total = lax.all_gather(block_in, 'item').sum(axis=0)  62.8 us
    reduce_sum x3, other arithmetic, col_reduce(): block_total = jnp.sum(jnp.exp(logits - block_peak[:, :, None, :]), axis=2)  62 us
    gather x8, local copies, waits for them, and re-layouts, build_tiles(): picked = code_column_splits[:, ids, :]  61.3 us
    all_gather x1, waiting for transfers between devices, body(): code_cols = lax.all_gather(codebook, 'item', axis=0, tiled=True)  52.7 us
  transfers between devices with their start and end apart: 2, of which 1 were waited for; matrix products, arithmetic and copies ran while one was open for 1% of the time, Pallas kernels for 0%

profile of v1, /device:TPU:0, one launch (start us, length us, event | category | flops | bytes accessed | tf_op | source)
XLA Modules:
  0.0 955.2 jit_solution(13780159387268010133)
XLA Ops:
  10.0 42.6 %psum.35 = f32[]{:T(128)} all-reduce(f32[]{:T(128)} %reduce_sum.99), channel_id=1, replica_groups=mesh['item'=16,'code'=8] {'item'}, use_global_device_ids=true, to_apply=%region_1.0 | all-reduce | flops 1 | bytes 8 | tf_op jit(solution)/shard_map/psum | solution.py:22
  58.9 5.6 copy.31
  64.6 52.7 %all-gather.6.cloned.1.call-done = f32[256,8192]{1,0:T(8,128)} async-done(((f32[16,8192]{1,0:T(8,128)}), f32[256,8192]{1,0:T(8,128)}) %all-gather.6.cloned.1.call-update) | async-done | bytes 8388624 | tf_op jit(solution)/shard_map/all_gather | solution.py:15
  117.3 9.0 copy.30
  126.3 158.7 %while.43 = (s32[]{:T(128)}, f32[8,8,16,64,64]{3,4,2,1,0:T(8,128)}, s32[8]{0:T(128)S(1)}, pred[64,16]{1,0:T(8,128)(4,1)S(1)}, s32[64,16]{1,0:T(8,128)S(1)}, /*in...) while((s32[]{:T(128)}, f32[8,8,16,64,64]{3,4,2,1,0:T(8,128)}, ...), condition=%wide.region_3.0_spmd, body=%wide.region_2.0_spmd.sunk | while | flops 1611662720 | bytes 29892660 | solution.py:51
  127.5 7.7 gather_fusion
  135.2 11.0 %bitcast_dynamic-update-slice_fusion.2 = f32[8,8,16,64,64]{3,4,2,1,0:T(8,128)} fusion(f32[8,8,16,64,64]{3,4,2,1,0:T(8,128)} %get-tuple-element.327, s32[]{:T(128)} %get-tuple-element.326, f32[256,8,16,64]{0,3,2,1:T(8,128)} %bitcast.84, pred[8,16]{1,0:T(8,128)(4,1)S(1)} %constant_dynamic-slice_fusion.2, f32[256,64,64]{0,2,1:T(8,128)} %get-tuple-element.343, ...), kind=kOutput, calls=%fused_computation.7.clone.1 | convolution fusion | flops 1611661312 | bytes 13107844 | tf_op jit(solution)/shard_map/while/body/eval_jaxpr/rbi,rbsj->bsij/dot_general | solution.py:37
  147.3 7.7 gather_fusion
  155.0 11.0 %bitcast_dynamic-update-slice_fusion.2 = f32[8,8,16,64,64]{3,4,2,1,0:T(8,128)} fusion(f32[8,8,16,64,64]{3,4,2,1,0:T(8,128)} %get-tuple-element.327, s32[]{:T(128)} %get-tuple-element.326, f32[256,8,16,64]{0,3,2,1:T(8,128)} %bitcast.84, pred[8,16]{1,0:T(8,128)(4,1)S(1)} %constant_dynamic-slice_fusion.2, f32[256,64,64]{0,2,1:T(8,128)} %get-tuple-element.343, ...), kind=kOutput, calls=%fused_computation.7.clone.1 | convolution fusion | flops 1611661312 | bytes 13107844 | tf_op jit(solution)/shard_map/while/body/eval_jaxpr/rbi,rbsj->bsij/dot_general | solution.py:37
  167.2 7.7 gather_fusion
  174.8 10.9 %bitcast_dynamic-update-slice_fusion.2 = f32[8,8,16,64,64]{3,4,2,1,0:T(8,128)} fusion(f32[8,8,16,64,64]{3,4,2,1,0:T(8,128)} %get-tuple-element.327, s32[]{:T(128)} %get-tuple-element.326, f32[256,8,16,64]{0,3,2,1:T(8,128)} %bitcast.84, pred[8,16]{1,0:T(8,128)(4,1)S(1)} %constant_dynamic-slice_fusion.2, f32[256,64,64]{0,2,1:T(8,128)} %get-tuple-element.343, ...), kind=kOutput, calls=%fused_computation.7.clone.1 | convolution fusion | flops 1611661312 | bytes 13107844 | tf_op jit(solution)/shard_map/while/body/eval_jaxpr/rbi,rbsj->bsij/dot_general | solution.py:37
  187.0 7.7 gather_fusion
  194.7 10.9 %bitcast_dynamic-update-slice_fusion.2 = f32[8,8,16,64,64]{3,4,2,1,0:T(8,128)} fusion(f32[8,8,16,64,64]{3,4,2,1,0:T(8,128)} %get-tuple-element.327, s32[]{:T(128)} %get-tuple-element.326, f32[256,8,16,64]{0,3,2,1:T(8,128)} %bitcast.84, pred[8,16]{1,0:T(8,128)(4,1)S(1)} %constant_dynamic-slice_fusion.2, f32[256,64,64]{0,2,1:T(8,128)} %get-tuple-element.343, ...), kind=kOutput, calls=%fused_computation.7.clone.1 | convolution fusion | flops 1611661312 | bytes 13107844 | tf_op jit(solution)/shard_map/while/body/eval_jaxpr/rbi,rbsj->bsij/dot_general | solution.py:37
  206.8 7.7 gather_fusion
  214.5 11.0 %bitcast_dynamic-update-slice_fusion.2 = f32[8,8,16,64,64]{3,4,2,1,0:T(8,128)} fusion(f32[8,8,16,64,64]{3,4,2,1,0:T(8,128)} %get-tuple-element.327, s32[]{:T(128)} %get-tuple-element.326, f32[256,8,16,64]{0,3,2,1:T(8,128)} %bitcast.84, pred[8,16]{1,0:T(8,128)(4,1)S(1)} %constant_dynamic-slice_fusion.2, f32[256,64,64]{0,2,1:T(8,128)} %get-tuple-element.343, ...), kind=kOutput, calls=%fused_computation.7.clone.1 | convolution fusion | flops 1611661312 | bytes 13107844 | tf_op jit(solution)/shard_map/while/body/eval_jaxpr/rbi,rbsj->bsij/dot_general | solution.py:37
  226.7 7.7 gather_fusion
  234.3 11.0 %bitcast_dynamic-update-slice_fusion.2 = f32[8,8,16,64,64]{3,4,2,1,0:T(8,128)} fusion(f32[8,8,16,64,64]{3,4,2,1,0:T(8,128)} %get-tuple-element.327, s32[]{:T(128)} %get-tuple-element.326, f32[256,8,16,64]{0,3,2,1:T(8,128)} %bitcast.84, pred[8,16]{1,0:T(8,128)(4,1)S(1)} %constant_dynamic-slice_fusion.2, f32[256,64,64]{0,2,1:T(8,128)} %get-tuple-element.343, ...), kind=kOutput, calls=%fused_computation.7.clone.1 | convolution fusion | flops 1611661312 | bytes 13107844 | tf_op jit(solution)/shard_map/while/body/eval_jaxpr/rbi,rbsj->bsij/dot_general | solution.py:37
  246.5 7.7 gather_fusion
  254.2 10.9 %bitcast_dynamic-update-slice_fusion.2 = f32[8,8,16,64,64]{3,4,2,1,0:T(8,128)} fusion(f32[8,8,16,64,64]{3,4,2,1,0:T(8,128)} %get-tuple-element.327, s32[]{:T(128)} %get-tuple-element.326, f32[256,8,16,64]{0,3,2,1:T(8,128)} %bitcast.84, pred[8,16]{1,0:T(8,128)(4,1)S(1)} %constant_dynamic-slice_fusion.2, f32[256,64,64]{0,2,1:T(8,128)} %get-tuple-element.343, ...), kind=kOutput, calls=%fused_computation.7.clone.1 | convolution fusion | flops 1611661312 | bytes 13107844 | tf_op jit(solution)/shard_map/while/body/eval_jaxpr/rbi,rbsj->bsij/dot_general | solution.py:37
  266.3 7.7 gather_fusion
  274.0 11.0 %bitcast_dynamic-update-slice_fusion.2 = f32[8,8,16,64,64]{3,4,2,1,0:T(8,128)} fusion(f32[8,8,16,64,64]{3,4,2,1,0:T(8,128)} %get-tuple-element.327, s32[]{:T(128)} %get-tuple-element.326, f32[256,8,16,64]{0,3,2,1:T(8,128)} %bitcast.84, pred[8,16]{1,0:T(8,128)(4,1)S(1)} %constant_dynamic-slice_fusion.2, f32[256,64,64]{0,2,1:T(8,128)} %get-tuple-element.343, ...), kind=kOutput, calls=%fused_computation.7.clone.1 | convolution fusion | flops 1611661312 | bytes 13107844 | tf_op jit(solution)/shard_map/while/body/eval_jaxpr/rbi,rbsj->bsij/dot_general | solution.py:37
  285.0 11.8 %add_reduce_fusion.5 = f32[8,8,64]{2,1,0:T(8,128)S(1)} fusion(f32[8,8,16,64,64]{3,4,2,1,0:T(8,128)} %get-tuple-element.105, f32[8,8,16,64]{3,2,1,0:T(8,128)S(1)} %bitcast.93), kind=kLoop, calls=%fused_computation.37 | loop fusion | flops 8384512 | bytes 17055744 | tf_op jit(solution)/shard_map/reduce_max | solution.py:70
  296.8 11.9 %exponential_reduce_fusion.5 = f32[8,8,64]{2,1,0:T(8,128)S(1)} fusion(f32[8,8,16,64,64]{3,4,2,1,0:T(8,128)} %get-tuple-element.105, f32[8,8,64]{2,1,0:T(8,128)S(1)} %add_reduce_fusion.5, f32[8,8,16,64]{3,2,1,0:T(8,128)S(1)} %bitcast.94), kind=kLoop, calls=%fused_computation.31 | loop fusion | flops 12578816 | bytes 17072128 | tf_op jit(solution)/shard_map/reduce_sum | solution.py:71
  308.9 25.5 %pmax.42 = f32[4096]{0:T(1024)S(1)} all-reduce(f32[4096]{0:T(1024)S(1)} %reshape.211), channel_id=1, replica_groups=mesh['item'=16,'code'=8] {'code'}, use_global_device_ids=true, to_apply=%region_7.8 | all-reduce | flops 4096 | bytes 32768 | tf_op jit(solution)/shard_map/pmax | solution.py:77
  334.4 24.6 %all-reduce.3 = (f32[4096]{0:T(1024)S(1)}, f32[]{:T(128)}) all-reduce(f32[4096]{0:T(1024)S(1)} %exponential_multiply_fusion.5, f32[]{:T(128)} %reduce_sum.100), channel_id=1, replica_groups=mesh['item'=16,'code'=8] {'code'}, use_global_device_ids=true, to_apply=%region_9.10 | all-reduce | flops 4097 | bytes 32776 | tf_op jit(solution)/shard_map/psum | solution.py:78
  359.1 15.3 %add_reduce_fusion.4 = f32[8,8,16,64]{3,2,1,0:T(8,128)S(1)} fusion(f32[8,8,16,64,64]{3,4,2,1,0:T(8,128)} %get-tuple-element.105, f32[8,8,64]{2,1,0:T(8,128)S(1)} %add.148), kind=kLoop, calls=%fused_computation.36 | loop fusion | flops 8323072 | bytes 17055744 | tf_op jit(solution)/shard_map/reduce_max | solution.py:84
  374.4 20.7 %exponential_reduce_fusion.4 = f32[8,8,16,64]{3,2,1,0:T(8,128)S(1)} fusion(f32[8,8,16,64,64]{3,4,2,1,0:T(8,128)} %get-tuple-element.105, f32[8,8,16,64]{3,2,1,0:T(8,128)S(1)} %add_reduce_fusion.4, f32[8,8,64]{2,1,0:T(8,128)S(1)} %add.148), kind=kLoop, calls=%fused_computation.30 | loop fusion | flops 12517376 | bytes 17317888 | tf_op jit(solution)/shard_map/reduce_sum | solution.py:85
  395.1 13.3 %while.44 = (s32[]{:T(128)}, f32[128,64]{0,1:T(8,128)S(1)}, pred[4,256,128]{2,1,0:T(8,128)(4,1)S(1)}, f32[4,256,64]{2,1,0:T(8,128)S(1)}, s32[]{:T(128)}, /*index=5*/s32[]{:T(128)}) while((s32[]{:T(128)}, f32[128,64]{0,1:T(8,128)S(1)}, pred[4,256,128]{2,1,0:T(8,128)(4,1)S(1)}, f32[4,256,64]{2,1,0:T(8,128)S(1)}, s32[]{:T(128)}, ...), condition=%wide.region_13.14_spmd.clone, body=%wide.region_11.13_spmd.clone.sunk | while | flops 4202499 | bytes 426071 | solution.py:98
  412.4 72.4 %pmax.43 = f32[8192]{0:T(1024)S(1)} all-reduce(f32[8192]{0:T(1024)S(1)} %reshape.213), channel_id=1, replica_groups=mesh['item'=16,'code'=8] {'item'}, use_global_device_ids=true, to_apply=%region_14.15 | all-reduce | flops 8192 | bytes 65536 | tf_op jit(solution)/shard_map/pmax | solution.py:115
  484.8 20.9 %all-gather = f32[131072]{0:T(1024)S(1)} all-gather(f32[8192]{0:T(1024)S(1)} %exponential_multiply_fusion.2), channel_id=2, replica_groups=mesh['item'=16,'code'=8] {'item'}, dimensions={0}, use_global_device_ids=true | all-gather | bytes 557056 | tf_op jit(solution)/shard_map/all_gather | solution.py:117
  509.5 11.8 %add_reduce_fusion.3 = f32[8,8,64]{2,1,0:T(8,128)S(1)} fusion(f32[8,8,16,64,64]{3,4,2,1,0:T(8,128)} %get-tuple-element.105, f32[8,8,16,64]{3,2,1,0:T(8,128)S(1)} %bitcast.97), kind=kLoop, calls=%fused_computation.35 | loop fusion | flops 8384512 | bytes 17055744 | tf_op jit(solution)/shard_map/reduce_max | solution.py:70
  521.3 11.9 %exponential_reduce_fusion.3 = f32[8,8,64]{2,1,0:T(8,128)S(1)} fusion(f32[8,8,16,64,64]{3,4,2,1,0:T(8,128)} %get-tuple-element.105, f32[8,8,64]{2,1,0:T(8,128)S(1)} %add_reduce_fusion.3, f32[8,8,16,64]{3,2,1,0:T(8,128)S(1)} %bitcast.98), kind=kLoop, calls=%fused_computation.29 | loop fusion | flops 12578816 | bytes 17072128 | tf_op jit(solution)/shard_map/reduce_sum | solution.py:71
  533.4 23.5 %pmax.44 = f32[4096]{0:T(1024)S(1)} all-reduce(f32[4096]{0:T(1024)S(1)} %reshape.219), channel_id=1, replica_groups=mesh['item'=16,'code'=8] {'code'}, use_global_device_ids=true, to_apply=%region_18.19 | all-reduce | flops 4096 | bytes 32768 | tf_op jit(solution)/shard_map/pmax | solution.py:77
  556.9 23.6 %psum.38 = f32[4096]{0:T(1024)S(1)} all-reduce(f32[4096]{0:T(1024)S(1)} %exponential_multiply_fusion.4), channel_id=1, replica_groups=mesh['item'=16,'code'=8] {'code'}, use_global_device_ids=true, to_apply=%region_20.21 | all-reduce | flops 4096 | bytes 32768 | tf_op jit(solution)/shard_map/psum | solution.py:78
  580.6 15.3 %add_reduce_fusion.2 = f32[8,8,16,64]{3,2,1,0:T(8,128)S(1)} fusion(f32[8,8,16,64,64]{3,4,2,1,0:T(8,128)} %get-tuple-element.105, f32[8,8,64]{2,1,0:T(8,128)S(1)} %add.157), kind=kLoop, calls=%fused_computation.34 | loop fusion | flops 8323072 | bytes 17055744 | tf_op jit(solution)/shard_map/reduce_max | solution.py:84
  595.9 20.7 %exponential_reduce_fusion.2 = f32[8,8,16,64]{3,2,1,0:T(8,128)S(1)} fusion(f32[8,8,16,64,64]{3,4,2,1,0:T(8,128)} %get-tuple-element.105, f32[8,8,16,64]{3,2,1,0:T(8,128)S(1)} %add_reduce_fusion.2, f32[8,8,64]{2,1,0:T(8,128)S(1)} %add.157), kind=kLoop, calls=%fused_computation.28 | loop fusion | flops 12517376 | bytes 17317888 | tf_op jit(solution)/shard_map/reduce_sum | solution.py:85
  616.6 13.3 %while.45 = (s32[]{:T(128)}, f32[128,64]{0,1:T(8,128)S(1)}, pred[4,256,128]{2,1,0:T(8,128)(4,1)S(1)}, f32[4,256,64]{2,1,0:T(8,128)S(1)}, s32[]{:T(128)}, /*index=5*/s32[]{:T(128)}) while((s32[]{:T(128)}, f32[128,64]{0,1:T(8,128)S(1)}, pred[4,256,128]{2,1,0:T(8,128)(4,1)S(1)}, f32[4,256,64]{2,1,0:T(8,128)S(1)}, s32[]{:T(128)}, ...), condition=%wide.region_24.25_spmd.clone, body=%wide.region_22.24_spmd.clone.sunk | while | flops 4202499 | bytes 426071 | solution.py:98
  633.8 72.1 %pmax.45 = f32[8192]{0:T(1024)S(1)} all-reduce(f32[8192]{0:T(1024)S(1)} %reshape.221), channel_id=1, replica_groups=mesh['item'=16,'code'=8] {'item'}, use_global_device_ids=true, to_apply=%region_25.26 | all-reduce | flops 8192 | bytes 65536 | tf_op jit(solution)/shard_map/pmax | solution.py:115
  705.9 20.9 %all-gather.1 = f32[131072]{0:T(1024)S(1)} all-gather(f32[8192]{0:T(1024)S(1)} %exponential_multiply_fusion.1), channel_id=3, replica_groups=mesh['item'=16,'code'=8] {'item'}, dimensions={0}, use_global_device_ids=true | all-gather | bytes 557056 | tf_op jit(solution)/shard_map/all_gather | solution.py:117
  730.0 11.8 %add_reduce_fusion.1 = f32[8,8,64]{2,1,0:T(8,128)S(1)} fusion(f32[8,8,16,64,64]{3,4,2,1,0:T(8,128)} %get-tuple-element.105, f32[8,8,16,64]{3,2,1,0:T(8,128)S(1)} %bitcast.95), kind=kLoop, calls=%fused_computation.33 | loop fusion | flops 8384512 | bytes 17055744 | tf_op jit(solution)/shard_map/reduce_max | solution.py:70
  741.8 11.9 %exponential_reduce_fusion.1 = f32[8,8,64]{2,1,0:T(8,128)S(1)} fusion(f32[8,8,16,64,64]{3,4,2,1,0:T(8,128)} %get-tuple-element.105, f32[8,8,64]{2,1,0:T(8,128)S(1)} %add_reduce_fusion.1, f32[8,8,16,64]{3,2,1,0:T(8,128)S(1)} %bitcast.96), kind=kLoop, calls=%fused_computation.27 | loop fusion | flops 12578816 | bytes 17072128 | tf_op jit(solution)/shard_map/reduce_sum | solution.py:71
  753.8 23.5 %pmax.46 = f32[4096]{0:T(1024)S(1)} all-reduce(f32[4096]{0:T(1024)S(1)} %reshape.226), channel_id=1, replica_groups=mesh['item'=16,'code'=8] {'code'}, use_global_device_ids=true, to_apply=%region_29.30 | all-reduce | flops 4096 | bytes 32768 | tf_op jit(solution)/shard_map/pmax | solution.py:77
  777.4 23.8 %psum.39 = f32[4096]{0:T(1024)S(1)} all-reduce(f32[4096]{0:T(1024)S(1)} %exponential_multiply_fusion.3), channel_id=1, replica_groups=mesh['item'=16,'code'=8] {'code'}, use_global_device_ids=true, to_apply=%region_31.32 | all-reduce | flops 4096 | bytes 32768 | tf_op jit(solution)/shard_map/psum | solution.py:78
  801.3 15.3 %add_reduce_fusion = f32[8,8,16,64]{3,2,1,0:T(8,128)S(1)} fusion(f32[8,8,16,64,64]{3,4,2,1,0:T(8,128)} %get-tuple-element.105, f32[8,8,64]{2,1,0:T(8,128)S(1)} %add.165), kind=kLoop, calls=%fused_computation.32 | loop fusion | flops 8323072 | bytes 17055744 | tf_op jit(solution)/shard_map/reduce_max | solution.py:84
  816.6 20.7 %exponential_reduce_fusion = f32[8,8,16,64]{3,2,1,0:T(8,128)S(1)} fusion(f32[8,8,16,64,64]{3,4,2,1,0:T(8,128)} %get-tuple-element.105, f32[8,8,16,64]{3,2,1,0:T(8,128)S(1)} %add_reduce_fusion, f32[8,8,64]{2,1,0:T(8,128)S(1)} %add.165), kind=kLoop, calls=%fused_computation.26 | loop fusion | flops 12517376 | bytes 17317888 | tf_op jit(solution)/shard_map/reduce_sum | solution.py:85
  837.3 13.3 %while.46 = (s32[]{:T(128)}, f32[128,64]{0,1:T(8,128)S(1)}, pred[4,256,128]{2,1,0:T(8,128)(4,1)S(1)}, f32[4,256,64]{2,1,0:T(8,128)S(1)}, s32[]{:T(128)}, /*index=5*/s32[]{:T(128)}) while((s32[]{:T(128)}, f32[128,64]{0,1:T(8,128)S(1)}, pred[4,256,128]{2,1,0:T(8,128)(4,1)S(1)}, f32[4,256,64]{2,1,0:T(8,128)S(1)}, s32[]{:T(128)}, ...), condition=%wide.region_35.36_spmd.clone, body=%wide.region_33.35_spmd.clone.sunk | while | flops 4202499 | bytes 426071 | solution.py:98
  854.5 72.1 %pmax.47 = f32[8192]{0:T(1024)S(1)} all-reduce(f32[8192]{0:T(1024)S(1)} %reshape.228), channel_id=1, replica_groups=mesh['item'=16,'code'=8] {'item'}, use_global_device_ids=true, to_apply=%region_36.37 | all-reduce | flops 8192 | bytes 65536 | tf_op jit(solution)/shard_map/pmax | solution.py:115
  926.6 20.9 %all-gather.2 = f32[131072]{0:T(1024)S(1)} all-gather(f32[8192]{0:T(1024)S(1)} %exponential_multiply_fusion), channel_id=4, replica_groups=mesh['item'=16,'code'=8] {'item'}, dimensions={0}, use_global_device_ids=true | all-gather | bytes 557056 | tf_op jit(solution)/shard_map/all_gather | solution.py:117
  (175 shorter events, 72.5 us)
Async XLA Ops:
  7.2 51.8 %all-gather.8.cloned.1.call-start = ((), (), s32[]{:S(2)}) async-start(), calls=%async_computation.1 | async-start | bytes 4718592 | tf_op jit(solution)/shard_map/all_gather | solution.py:14
  7.9 109.4 %all-gather.6.cloned.1.call-start = ((), (), s32[]{:S(2)}) async-start(), calls=%async_computation | async-start | bytes 8912896 | tf_op jit(solution)/shard_map/all_gather | solution.py:15
  285.0 74.0 %copy-start.3 = (f32[4096]{0:T(1024)S(1)}, f32[4096]{0:T(1024)}, u32[]{:S(2)}) copy-start(f32[4096]{0:T(1024)} %param.15) | copy-start | bytes 49156
  359.1 147.5 %copy-start.2 = (f32[8192]{0:T(1024)S(1)}, f32[8192]{0:T(1024)}, u32[]{:S(2)}) copy-start(f32[8192]{0:T(1024)} %param.16) | copy-start | bytes 98308
  580.6 36.0 %copy-start.1 = (f32[128,64]{0,1:T(8,128)S(1)}, f32[128,64]{0,1:T(8,128)}, u32[]{:S(2)}) copy-start(f32[128,64]{0,1:T(8,128)} %custom-call.1) | copy-start | bytes 98308
  801.2 36.1 %copy-start.4 = (f32[4096]{0:T(1024)}, f32[4096]{0:T(1024)S(1)}, u32[]{:S(2)}) copy-start(f32[4096]{0:T(1024)S(1)} %add_subtract_fusion.3) | copy-start | bytes 49156
  801.3 36.0 %copy-start = (f32[128,64]{0,1:T(8,128)S(1)}, f32[128,64]{0,1:T(8,128)}, u32[]{:S(2)}) copy-start(f32[128,64]{0,1:T(8,128)} %custom-call.2) | copy-start | bytes 98308
Sparse Core Ops, SparseCore 0:
  9.7 34.5 all-gather.7
  46.4 70.8 all-gather.5
